TPU v7x, 32 devices: a whole 2x2x4 slice. The times are simulated.
32 devices in a mesh: group: 2 (over y), row: 4 (over z), col: 4 (over x, core).
Axes of the slice: x: 2, y: 2, z: 4, core: 2. Of those that a mesh axis runs over, the one named last changes fastest.
Arguments:
- pair: bfloat16 [1024, 512, 128], P(('group', 'row'), 'col'), parts along dimension 0, may hold values from -6 to 6
- chain_ids: int32 [1024], P('group'), parts along dimension 0, may hold values from 0 to 5, never falling along the last dimension, each value on 1 to 256 neighbouring positions
- block_mask: int32 [8, 4], P('group'), parts along dimension 0, may hold values 0 or 1
- norm_gain: float32 [2, 128], replicated, may hold values from 0.1 to 1.9
- norm_bias: float32 [2, 128], replicated, may hold values from -3 to 3
- proj_weight: bfloat16 [2, 128, 512], replicated, may hold values from -0.5 to 0.5
- gate_weight: bfloat16 [2, 128, 128], replicated, may hold values from -0.5 to 0.5
- out_gain: float32 [2, 128], replicated, may hold values from 0.1 to 1.9
- out_bias: float32 [2, 128], replicated, may hold values from -3 to 3
- out_weight: bfloat16 [2, 128, 128], replicated, may hold values from -0.5 to 0.5
Outputs:
- updated: bfloat16 [1024, 512, 128], P(('group', 'row'), 'col'), parts along dimension 0
There are 2 independent parts, one for each index of `group`. A program takes and returns all parts, laid end to end along the dimension named above; an argument that names none is the same for every part. Nothing has to cross between parts.
Inputs may be any that keep to these rules, and one draw needn't show every extreme that they name: `chain_ids`: chain ids never fall along the tokens; each chain holds 1 to 256 tokens, one chain exactly 256.
All inputs are finite; a program needn't handle non-finite values.
Results may differ from a plain program's by a relative error of at most 0.0095.
Values may be sent and summed in bfloat16 or wider, within the bound.
A program may use at most 192 MiB of HBM per device.

v0:
```python
import jax
import jax.numpy as jnp
from jax import lax
from jax.sharding import PartitionSpec as P

BLOCK = 128


EPSILON = 1e-05


def layer_norm(values, norm_gain, norm_shift):
    center = values - jnp.mean(values, axis=-1, keepdims=True)
    spread = jnp.mean(center * center, axis=-1, keepdims=True)
    return center * lax.rsqrt(spread + EPSILON) * norm_gain + norm_shift


def mask_tile(chain_ids, block_mask, tile_rows, tile_cols):
    row_start = lax.axis_index("row") * tile_rows
    col_start = lax.axis_index("col") * tile_cols
    row_tokens = row_start + jnp.arange(tile_rows, dtype=jnp.int32)
    col_tokens = col_start + jnp.arange(tile_cols, dtype=jnp.int32)
    row_chain = lax.dynamic_slice_in_dim(chain_ids, row_start, tile_rows)
    col_chain = lax.dynamic_slice_in_dim(chain_ids, col_start, tile_cols)
    block_ids = jnp.arange(block_mask.shape[0], dtype=jnp.int32)
    row_onehot = (row_tokens[:, None] // BLOCK == block_ids[None, :]).astype(jnp.float32)
    col_onehot = (col_tokens[:, None] // BLOCK == block_ids[None, :]).astype(jnp.float32)
    row_blocks = jnp.dot(
        row_onehot, block_mask.astype(jnp.float32), precision=lax.Precision.HIGHEST
    )
    block_tile = jnp.dot(row_blocks, col_onehot.T, precision=lax.Precision.HIGHEST)
    same_chain = (row_chain[:, None] == col_chain[None, :]).astype(jnp.float32)
    return jnp.maximum(same_chain, block_tile)


def panels_outgoing(left_side, right_side):
    tile_cols = left_side.shape[1]
    right_panel = lax.all_gather(right_side, "row", axis=0, tiled=True)

    def partial_sum(offset, amount):
        return jnp.einsum(
            "jkh,ikh->jih", right_panel, left_side, preferred_element_type=jnp.float32
        )

    summed = lax.psum_scatter(
        partial_sum(jnp.int32(0), lax.axis_size("col") * tile_cols).astype(jnp.bfloat16),
        "col",
        scatter_dimension=0,
        tiled=True,
    ).astype(jnp.float32)
    return jnp.transpose(summed, (1, 0, 2))


def panels_incoming(left_side, right_side):
    tile_rows = left_side.shape[0]
    left_panel = lax.all_gather(left_side, "col", axis=1, tiled=True)

    def partial_sum(offset, amount):
        return jnp.einsum(
            "kih,kjh->ijh", left_panel, right_side, preferred_element_type=jnp.float32
        )

    return lax.psum_scatter(
        partial_sum(jnp.int32(0), lax.axis_size("row") * tile_rows).astype(jnp.bfloat16),
        "row",
        scatter_dimension=0,
        tiled=True,
    ).astype(jnp.float32)


def triangle_sums(left_side, right_side, outgoing):
    if outgoing:
        return panels_outgoing(left_side, right_side)
    return panels_incoming(left_side, right_side)


def run_pass(
    state,
    pair_mask,
    norm_gain,
    norm_bias,
    proj_weight,
    gate_weight,
    out_gain,
    out_bias,
    out_weight,
    which_pass,
    outgoing,
):
    hidden = out_gain.shape[1]
    widened = state.astype(jnp.float32)
    normed = layer_norm(widened, norm_gain[which_pass], norm_bias[which_pass]).astype(jnp.bfloat16)
    projected = jnp.dot(normed, proj_weight[which_pass], preferred_element_type=jnp.float32)
    masked = pair_mask[:, :, None]
    left_side = (
        masked * jax.nn.sigmoid(projected[:, :, :hidden]) * projected[:, :, hidden : 2 * hidden]
    ).astype(jnp.bfloat16)
    right_side = (
        masked
        * jax.nn.sigmoid(projected[:, :, 2 * hidden : 3 * hidden])
        * projected[:, :, 3 * hidden :]
    ).astype(jnp.bfloat16)
    triangle = triangle_sums(left_side, right_side, outgoing)
    tri_normed = layer_norm(triangle, out_gain[which_pass], out_bias[which_pass]).astype(
        jnp.bfloat16
    )
    gating = jax.nn.sigmoid(
        jnp.dot(normed, gate_weight[which_pass], preferred_element_type=jnp.float32)
    )
    update = gating * jnp.dot(
        tri_normed, out_weight[which_pass], preferred_element_type=jnp.float32
    )
    return (widened + update).astype(jnp.bfloat16)


def local(
    pair,
    chain_ids,
    block_mask,
    norm_gain,
    norm_bias,
    proj_weight,
    gate_weight,
    out_gain,
    out_bias,
    out_weight,
):
    tile_rows, tile_cols = (pair.shape[0], pair.shape[1])
    pair_mask = mask_tile(chain_ids, block_mask, tile_rows, tile_cols)
    middle = run_pass(
        pair,
        pair_mask,
        norm_gain,
        norm_bias,
        proj_weight,
        gate_weight,
        out_gain,
        out_bias,
        out_weight,
        0,
        True,
    )
    return run_pass(
        middle,
        pair_mask,
        norm_gain,
        norm_bias,
        proj_weight,
        gate_weight,
        out_gain,
        out_bias,
        out_weight,
        1,
        False,
    )


def solution(mesh):
    placed = (
        P(("group", "row"), "col", None),
        P("group"),
        P("group", None),
        P(),
        P(),
        P(),
        P(),
        P(),
        P(),
        P(),
    )
    return jax.shard_map(
        local,
        mesh=mesh,
        in_specs=placed,
        out_specs=P(("group", "row"), "col", None),
        check_vma=False,
    )
```

profile of v0, /device:TPU:1, one launch (start us, length us, event | category | flops | bytes accessed | tf_op | source)
XLA Modules:
  0.0 1145.6 jit_solution(11199707176316778297)
XLA Ops:
  6.6 6.4 copy.68
  21.1 15.4 %fusion.56 = f32[128,128,512]{1,2,0:T(8,128)} fusion(bf16[2,128,512]{2,1,0:T(8,128)(2,1)S(1)} %copy-done.3, bf16[128,128,128]{1,2,0:T(8,128)(2,1)} %copy.68, f32[128]{0:T(128)S(1)} %get-tuple-element.18, f32[128]{0:T(128)S(1)} %get-tuple-element.21, f32[128,128]{1,0:T(8,128)S(1)} %add_rsqrt_fusion.3, f32[128,128]{1,0:T(8,128)S(1)} %broadcast_multiply_fusion.3), kind=kOutput, calls=%fused_computation.77 | convolution fusion | flops 2160066560 | bytes 38011904 | tf_op jit(solution)/shard_map/dot_general | solution.py:93
  36.5 16.0 %fusion.39 = (bf16[128,128,128]{1,2,0:T(8,128)(2,1)}, bf16[128,128,128]{1,2,0:T(8,128)(2,1)}) fusion(f32[128,128,512]{1,2,0:T(8,128)} %fusion.56, f32[128,128]{1,0:T(8,128)S(1)} %convolution_maximum_fusion), kind=kLoop, calls=%fused_computation.56 | loop fusion | flops 25165824 | bytes 42008576 | tf_op jit(solution)/shard_map/convert_element_type | solution.py:97
  52.5 6.4 copy.76
  59.3 288.8 %all-gather.3.cloned.1.call-done = bf16[512,128,128]{2,1,0:T(8,128)(2,1)} async-done(((bf16[128,128,128]{2,1,0:T(8,128)(2,1)}), bf16[512,128,128]{2,1,0:T(8,128)(2,1)}) %all-gather.3.cloned.1.call-update) | async-done | bytes 16777232 | tf_op jit(solution)/shard_map/all_gather | solution.py:38
  348.1 21.6 %copy.78 = bf16[512,128,128]{1,0,2:T(8,128)(2,1)} copy(bf16[512,128,128]{2,1,0:T(8,128)(2,1)} %all-gather.3.cloned.1.call-done) | data formatting | bytes 33554432 | tf_op jit(solution)/shard_map/all_gather | solution.py:38
  369.7 15.8 %convert_bitcast_fusion.1 = bf16[512,128,128]{0,1,2:T(8,128)(2,1)} fusion(bf16[512,128,128]{1,0,2:T(8,128)(2,1)} %copy.78, bf16[128,128,128]{1,2,0:T(8,128)(2,1)} %get-tuple-element.7), kind=kOutput, calls=%fused_computation.5 | convolution fusion | flops 2155872256 | bytes 37748736 | tf_op jit(solution)/shard_map/jkh,ikh->jih/dot_general | solution.py:41
  385.6 23.7 %copy.105 = bf16[512,128,128]{1,2,0:T(8,128)(2,1)} copy(bf16[512,128,128]{0,1,2:T(8,128)(2,1)} %convert_bitcast_fusion.1) | data formatting | bytes 33554432
  409.3 19.3 %copy.128 = bf16[64,8,128,128]{3,1,2,0:T(8,128)(2,1)} copy(bf16[64,8,128,128]{3,2,1,0:T(8,128)(2,1)} %bitcast.88) | data formatting | bytes 33554432
  429.3 123.5 %reduce-scatter.7.cloned.1.call-done = bf16[128,16384]{1,0:T(8,128)(2,1)} async-done(((bf16[512,16384]{1,0:T(8,128)(2,1)}), bf16[128,16384]{1,0:T(8,128)(2,1)}) %reduce-scatter.7.cloned.1.call-update) | async-done | bytes 4194320
  552.8 5.4 copy.112
  558.2 6.9 copy.106
  583.6 24.4 %fusion.54 = f32[128,128,512]{1,2,0:T(8,128)} fusion(bf16[2,128,512]{2,1,0:T(8,128)(2,1)S(1)} %copy-done.3, bf16[128,128,128]{1,2,0:T(8,128)(2,1)S(1)} %get-tuple-element.20, f32[128]{0:T(128)S(1)} %get-tuple-element.17, f32[128]{0:T(128)S(1)} %get-tuple-element.22, f32[128,128]{1,0:T(8,128)S(1)} %add_rsqrt_fusion.1, ...), kind=kOutput, calls=%fused_computation.75 | convolution fusion | flops 2160066560 | bytes 38011904 | tf_op jit(solution)/shard_map/dot_general | solution.py:93
  607.9 16.0 %fusion.29 = (bf16[128,128,128]{1,2,0:T(8,128)(2,1)}, bf16[128,128,128]{1,2,0:T(8,128)(2,1)}) fusion(f32[128,128,512]{1,2,0:T(8,128)} %fusion.54, f32[128,128]{1,0:T(8,128)S(1)} %convolution_maximum_fusion), kind=kLoop, calls=%fused_computation.42 | loop fusion | flops 25165824 | bytes 42008576 | tf_op jit(solution)/shard_map/convert_element_type | solution.py:102
  624.0 108.7 %all-gather.5.cloned.1.call-done = bf16[128,512,128]{1,2,0:T(8,128)(2,1)} async-done(((bf16[128,128,128]{1,2,0:T(8,128)(2,1)}), bf16[128,512,128]{1,2,0:T(8,128)(2,1)}) %all-gather.5.cloned.1.call-update) | async-done | bytes 16777232 | tf_op jit(solution)/shard_map/all_gather | solution.py:56
  732.7 35.2 %convert_bitcast_fusion = bf16[512,128,128]{0,1,2:T(8,128)(2,1)} fusion(bf16[128,512,128]{1,2,0:T(8,128)(2,1)} %all-gather.5.cloned.1.call-done, bf16[128,128,128]{1,2,0:T(8,128)(2,1)} %get-tuple-element.5), kind=kOutput, calls=%fused_computation.4 | convolution fusion | flops 2155872256 | bytes 37748736 | tf_op jit(solution)/shard_map/kih,kjh->ijh/dot_general | solution.py:59
  767.9 23.6 %copy.107 = bf16[512,128,128]{1,2,0:T(8,128)(2,1)} copy(bf16[512,128,128]{0,1,2:T(8,128)(2,1)} %convert_bitcast_fusion) | data formatting | bytes 33554432
  791.5 19.3 %copy.127 = bf16[64,8,128,128]{3,1,2,0:T(8,128)(2,1)} copy(bf16[64,8,128,128]{3,2,1,0:T(8,128)(2,1)} %bitcast.89) | data formatting | bytes 33554432
  810.9 7.7 fusion.64
  818.6 272.2 %reduce-scatter.9.cloned.1.call-done = bf16[128,16384]{1,0:T(8,128)(2,1)} async-done(((bf16[512,16384]{1,0:T(8,128)(2,1)}), bf16[128,16384]{1,0:T(8,128)(2,1)}) %reduce-scatter.9.cloned.1.call-update) | async-done | bytes 4194320
  1096.1 6.9 copy.108
  1114.4 7.3 copy.94
  1121.6 10.8 fusion.23
  1132.5 6.4 copy.96
  (62 shorter events, 44.2 us)
Async XLA Ops:
  6.5 341.6 %all-gather.3.cloned.1.call-start = ((), (), s32[]{:S(2)}) async-start(), calls=%async_computation.2 | async-start | bytes 20971520 | tf_op jit(solution)/shard_map/all_gather | solution.py:38
  6.5 13.9 %copy-start.11 = (s32[4,4]{1,0:T(4,128)S(1)}, s32[4,4]{1,0:T(4,128)}, u32[]{:S(2)}) copy-start(s32[4,4]{1,0:T(4,128)} %param.12) | copy-start | bytes 196
  6.6 14.0 %copy-start.6 = (f32[2,128]{1,0:T(2,128)S(1)}, f32[2,128]{1,0:T(2,128)}, u32[]{:S(2)}) copy-start(f32[2,128]{1,0:T(2,128)} %param.14) | copy-start | bytes 3076
  6.6 14.0 %copy-start.7 = (f32[2,128]{1,0:T(2,128)S(1)}, f32[2,128]{1,0:T(2,128)}, u32[]{:S(2)}) copy-start(f32[2,128]{1,0:T(2,128)} %param.13) | copy-start | bytes 3076
  6.6 14.1 %copy-start.10 = (s32[512]{0:T(512)S(1)}, s32[512]{0:T(512)}, u32[]{:S(2)}) copy-start(s32[512]{0:T(512)} %param.11) | copy-start | bytes 6148
  6.6 14.5 %copy-start.3 = (bf16[2,128,512]{2,1,0:T(8,128)(2,1)S(1)}, bf16[2,128,512]{2,1,0:T(8,128)(2,1)}, u32[]{:S(2)}) copy-start(bf16[2,128,512]{2,1,0:T(8,128)(2,1)} %param.15) | copy-start | bytes 786436
  58.9 493.9 %reduce-scatter.7.cloned.1.call-start = ((), (), s32[]{:S(2)}) async-start(), calls=%async_computation.4 | async-start | bytes 20971520
  428.6 0.7 copy-start.8
  428.6 0.7 copy-start.9
  428.6 304.1 %all-gather.5.cloned.1.call-start = ((), (), s32[]{:S(2)}) async-start(), calls=%async_computation.3 | async-start | bytes 20971520 | tf_op jit(solution)/shard_map/all_gather | solution.py:56
  565.1 6.3 copy-start
  565.1 8.3 copy-start.5
  573.5 3.2 copy-start.1
  573.5 3.2 copy-start.4
  581.8 26.2 %copy-start.2 = (bf16[128,128,128]{1,2,0:T(8,128)(2,1)}, bf16[128,128,128]{1,2,0:T(8,128)(2,1)S(1)}, u32[]{:S(2)}) copy-start(bf16[128,128,128]{1,2,0:T(8,128)(2,1)S(1)} %get-tuple-element.20) | copy-start | bytes 12582916
  624.0 466.8 %reduce-scatter.9.cloned.1.call-start = ((), (), s32[]{:S(2)}) async-start(), calls=%async_computation.5 | async-start | bytes 20971520
Sparse Core Ops, SparseCore 0:
  59.0 289.0 all-gather.2
  428.7 124.0 reduce-scatter.6
  624.1 108.5 all-gather.4
  811.0 279.7 reduce-scatter.8
where the time goes:
time: 1150 us
  waiting for transfers between devices  793 us (69%)
  local copies, waits for them, and re-layouts  160 us (14%)
  matrix products  118 us (10%)
  other arithmetic  60.4 us (5%)
  between operations  13.6 us (1%)
    unnamed x6, waiting for transfers between devices  396 us
    all_gather x1, waiting for transfers between devices, panels_outgoing(): right_panel = lax.all_gather(right_side, 'row', axis=0, tiled=True)  289 us
    unnamed x33, local copies, waits for them, and re-layouts  118 us
    all_gather x1, waiting for transfers between devices, panels_incoming(): left_panel = lax.all_gather(left_side, 'col', axis=1, tiled=True)  109 us
    dot_general x2, matrix products, run_pass(): jnp.dot(normed, proj_weight[which_pass], preferred_element_type=jnp.float32)  39.8 us
    dot_general x1, matrix products, partial_sum(): jnp.einsum('kih,kjh->ijh', left_panel, right_side, preferred_element_type...  35.2 us
  transfers between devices with their start and end apart: 4, of which 4 were waited for; matrix products, arithmetic and copies ran while one was open for 1% of the time, Pallas kernels for 0%

commit v1 on v0

--- a/solution.py
+++ b/solution.py
@@ -1,6 +1,10 @@
+import functools
+
 import jax
 import jax.numpy as jnp
 from jax import lax
+from jax.experimental import pallas as pl
+from jax.experimental.pallas import tpu as pltpu
 from jax.sharding import PartitionSpec as P
 
 BLOCK = 128
@@ -68,7 +72,301 @@
     ).astype(jnp.float32)
 
 
+MESH = pl.DeviceIdType.MESH
+CHUNKS = 8
+
+
+def triangle_kernel(
+    outgoing, half, step, moved_ref, fixed_ref, out_ref, moved, fixed, summed, landed, sent,
+    ready, local_sem, send_moved, recv_moved, send_fixed, recv_fixed, send_peer, recv_peer,
+    send_relay, recv_relay, send_sum, recv_sum, send_out, recv_out,
+):
+    row, col = lax.axis_index("row"), lax.axis_index("col")
+    side, place = row // 2, row % 2
+    across, core = col // 2, col % 2
+    hub = (row == 1) | (row == 2)
+    edge = jnp.logical_not(hub)
+    hub_row = side + 1
+    end_row = 3 * side
+    end_place = side
+    hub_place = 1 - side
+    other = 1 - core
+    pair_at = {"row": row, "col": 2 * across + other}
+    if outgoing:
+        slot = (row, core)
+        held = (place, core)
+        mine = across
+        peer = [{"row": 3 - row, "col": 2 * across + b} for b in range(2)]
+        peer_same = {"row": 3 - row, "col": col}
+        sum_peer = {"row": row, "col": 2 * (1 - across) + core}
+        moved_pair, fixed_pair = (row, other), (place, other)
+        moved_end = [(end_row, b) for b in range(2)]
+        fixed_end = [(end_place, b) for b in range(2)]
+        moved_peer = [(3 - row, b) for b in range(2)]
+    else:
+        slot = (col, place)
+        held = (core, place)
+        mine = side
+        peer = [{"row": row, "col": 2 * (1 - across) + b} for b in range(2)]
+        peer_same = {"row": row, "col": 2 * (1 - across) + core}
+        sum_peer = {"row": 3 - row, "col": col}
+        moved_pair, fixed_pair = (2 * across + other, place), (other, place)
+        moved_end = [(2 * across + b, end_place) for b in range(2)]
+        fixed_end = [(b, end_place) for b in range(2)]
+        moved_peer = [(2 * (1 - across) + b, place) for b in range(2)]
+    hub_at = [{"row": hub_row, "col": 2 * across + b} for b in range(2)]
+    end_at = [{"row": end_row, "col": 2 * across + b} for b in range(2)]
+
+    def remote(source, target, send, recv, device):
+        return pltpu.make_async_remote_copy(
+            src_ref=source, dst_ref=target, send_sem=send, recv_sem=recv,
+            device_id=device, device_id_type=MESH,
+        )
+
+    def part(g):
+        return pl.ds(g * step, step)
+
+    def span(half_of, g):
+        return pl.ds(half_of * half + g * step, step)
+
+    def swap_moved(g):
+        return remote(moved_ref.at[span(other, g)], moved.at[slot[0], slot[1], part(g)],
+                      send_moved.at[0, g], recv_moved.at[0, g], pair_at)
+
+    def swap_fixed(g):
+        return remote(fixed_ref.at[span(other, g)], fixed.at[held[0], held[1], part(g)],
+                      send_fixed.at[0, g], recv_fixed.at[0, g], pair_at)
+
+    def end_moved(g, b):
+        return remote(moved_ref.at[span(b, g)], moved.at[slot[0], slot[1], part(g)],
+                      send_moved.at[b, g], recv_moved.at[1 + core, g], hub_at[b])
+
+    def end_fixed(g, b):
+        return remote(fixed_ref.at[span(b, g)], fixed.at[held[0], held[1], part(g)],
+                      send_fixed.at[b, g], recv_fixed.at[1 + core, g], hub_at[b])
+
+    def to_peer(g, b):
+        return remote(moved_ref.at[span(b, g)], moved.at[slot[0], slot[1], part(g)],
+                      send_peer.at[b, g], recv_peer.at[core, g], peer[b])
+
+    def relay_view(g, there):
+        if outgoing:
+            return moved.at[3 - end_row if there else end_row, :, part(g)]
+        start = 2 * (1 - across if there else across)
+        return moved.at[pl.ds(start, 2), end_place, part(g)]
+
+    def relay(g):
+        return remote(relay_view(g, False), relay_view(g, False),
+                      send_relay.at[g], recv_relay.at[g], peer_same)
+
+    def arrived(view, sem):
+        remote(view, view, send_relay.at[0], sem, pair_at).wait_recv()
+
+    def sums_to(g):
+        return remote(sent.at[g % 2], landed.at[part(g)], send_sum.at[g], recv_sum.at[g], sum_peer)
+
+    def result_pair(g):
+        return remote(ready.at[g % 2, hub_place, other], out_ref.at[span(core, g)],
+                      send_out.at[2, g], recv_out.at[core, g], pair_at)
+
+    def result_end(g, b):
+        return remote(ready.at[g % 2, end_place, b], out_ref.at[span(core, g)],
+                      send_out.at[b, g], recv_out.at[core, g], end_at[b])
+
+    barrier = pltpu.get_barrier_semaphore()
+
+    @pl.when(hub)
+    def _():
+        for device in [pair_at, sum_peer] + end_at + peer:
+            pl.semaphore_signal(barrier, inc=1, device_id=device, device_id_type=MESH)
+        pl.semaphore_wait(barrier, 6)
+
+    @pl.when(edge)
+    def _():
+        for device in hub_at:
+            pl.semaphore_signal(barrier, inc=1, device_id=device, device_id_type=MESH)
+        pl.semaphore_wait(barrier, 2)
+
+    def tile(group, e, b, h):
+        total = None
+        for v in range(2):
+            if outgoing:
+                lhs, rhs = fixed[e, v, h], moved[2 * group + b, v, h]
+            else:
+                lhs, rhs = moved[2 * group + e, v, h], fixed[b, v, h]
+            term = jnp.dot(lhs, rhs, preferred_element_type=jnp.float32)
+            total = term if total is None else total + term
+        return total
+
+    @pl.when(edge)
+    def _():
+        for g in range(CHUNKS):
+            if g >= 2:
+                for b in range(2):
+                    end_moved(g - 2, b).wait_send()
+                    end_fixed(g - 2, b).wait_send()
+            for b in range(2):
+                end_moved(g, b).start()
+            for b in range(2):
+                end_fixed(g, b).start()
+        for g in range(CHUNKS - 2, CHUNKS):
+            for b in range(2):
+                end_moved(g, b).wait_send()
+                end_fixed(g, b).wait_send()
+        for g in range(CHUNKS):
+            for b in range(2):
+                arrived(out_ref.at[span(b, g)], recv_out.at[b, g])
+
+    @pl.when(hub)
+    def _():
+        own = [
+            pltpu.make_async_copy(moved_ref.at[pl.ds(core * half, half)],
+                                  moved.at[slot[0], slot[1]], local_sem.at[0]),
+            pltpu.make_async_copy(fixed_ref.at[pl.ds(core * half, half)],
+                                  fixed.at[held[0], held[1]], local_sem.at[1]),
+        ]
+
+        def begin(g):
+            for b in range(2):
+                to_peer(g, b).start()
+            swap_moved(g).start()
+            swap_fixed(g).start()
+
+        begin(0)
+        for copy in own:
+            copy.start()
+        begin(1)
+        for copy in own:
+            copy.wait()
+        for g in range(CHUNKS + 2):
+            if 2 <= g + 1 < CHUNKS:
+                begin(g + 1)
+            if g < CHUNKS:
+                for b in range(2):
+                    u, v = moved_end[b]
+                    arrived(moved.at[u, v, part(g)], recv_moved.at[1 + b, g])
+                relay(g).start()
+            n = g - 1
+            if 0 <= n < CHUNKS:
+                for b in range(2):
+                    u, v = fixed_end[b]
+                    arrived(fixed.at[u, v, part(n)], recv_fixed.at[1 + b, n])
+                    u, v = moved_peer[b]
+                    arrived(moved.at[u, v, part(n)], recv_peer.at[b, n])
+                arrived(moved.at[moved_pair[0], moved_pair[1], part(n)], recv_moved.at[0, n])
+                arrived(fixed.at[fixed_pair[0], fixed_pair[1], part(n)], recv_fixed.at[0, n])
+                arrived(relay_view(n, True), recv_relay.at[n])
+                if n >= 2:
+                    sums_to(n - 2).wait_send()
+
+                @pl.loop(0, step)
+                def _(h):
+                    for e in range(2):
+                        for b in range(2):
+                            sent[n % 2, h, e, b] = tile(1 - mine, e, b, n * step + h).astype(
+                                jnp.bfloat16
+                            )
+
+                sums_to(n).start()
+
+                @pl.loop(0, step)
+                def _(h):
+                    for e in range(2):
+                        for b in range(2):
+                            summed[n % 2, h, e, b] = tile(mine, e, b, n * step + h)
+
+            n = g - 2
+            if 0 <= n < CHUNKS:
+                arrived(landed.at[part(n)], recv_sum.at[n])
+                if n >= 2:
+                    result_pair(n - 2).wait_send()
+                    for b in range(2):
+                        result_end(n - 2, b).wait_send()
+
+                @pl.loop(0, step)
+                def _(h):
+                    for e in range(2):
+                        for b in range(2):
+                            ready[n % 2, e, b, h] = (
+                                summed[n % 2, h, e, b]
+                                + landed[n * step + h, e, b].astype(jnp.float32)
+                            ).astype(jnp.bfloat16)
+                    out_ref[core * half + n * step + h] = ready[n % 2, hub_place, core, h]
+
+                for b in range(2):
+                    result_end(n, b).start()
+                result_pair(n).start()
+        for g in range(CHUNKS):
+            for b in range(2):
+                to_peer(g, b).wait_send()
+            swap_moved(g).wait_send()
+            swap_fixed(g).wait_send()
+            relay(g).wait_send()
+        for g in range(CHUNKS - 2, CHUNKS):
+            sums_to(g).wait_send()
+            result_pair(g).wait_send()
+            for b in range(2):
+                result_end(g, b).wait_send()
+        for g in range(CHUNKS):
+            arrived(out_ref.at[span(other, g)], recv_out.at[other, g])
+
+
+def hub_sums(left_side, right_side, outgoing):
+    moved, fixed = (right_side, left_side) if outgoing else (left_side, right_side)
+    hidden, edge = moved.shape[0], moved.shape[1]
+    half = hidden // 2
+    step = half // CHUNKS
+    tile = (edge, edge)
+    sem = pltpu.SemaphoreType.DMA
+    return pl.pallas_call(
+        functools.partial(triangle_kernel, outgoing, half, step),
+        out_shape=jax.ShapeDtypeStruct(moved.shape, jnp.bfloat16),
+        in_specs=[pl.BlockSpec(memory_space=pl.ANY)] * 2,
+        out_specs=pl.BlockSpec(memory_space=pltpu.VMEM),
+        scratch_shapes=[
+            pltpu.VMEM((4, 2, half) + tile, jnp.bfloat16),
+            pltpu.VMEM((2, 2, half) + tile, jnp.bfloat16),
+            pltpu.VMEM((2, step, 2, 2) + tile, jnp.float32),
+            pltpu.VMEM((half, 2, 2) + tile, jnp.bfloat16),
+            pltpu.VMEM((2, step, 2, 2) + tile, jnp.bfloat16),
+            pltpu.VMEM((2, 2, 2, step) + tile, jnp.bfloat16),
+            sem((2,)),
+            sem((2, CHUNKS)), sem((3, CHUNKS)),
+            sem((2, CHUNKS)), sem((3, CHUNKS)),
+            sem((2, CHUNKS)), sem((2, CHUNKS)),
+            sem((CHUNKS,)), sem((CHUNKS,)),
+            sem((CHUNKS,)), sem((CHUNKS,)),
+            sem((3, CHUNKS)), sem((2, CHUNKS)),
+        ],
+        compiler_params=pltpu.CompilerParams(
+            collective_id=0 if outgoing else 1,
+            has_side_effects=True,
+            vmem_limit_bytes=56 * 1024 * 1024,
+        ),
+        cost_estimate=pl.CostEstimate(
+            flops=32 * hidden * edge**3, bytes_accessed=6 * hidden * edge * edge, transcendentals=0
+        ),
+    )(moved, fixed)
+
+
+def takes_hubs(left_side):
+    rows, cols, hidden = left_side.shape
+    return (
+        lax.axis_size("row") == 4
+        and lax.axis_size("col") == 4
+        and rows == cols
+        and rows % 128 == 0
+        and hidden % (2 * CHUNKS) == 0
+    )
+
+
 def triangle_sums(left_side, right_side, outgoing):
+    if takes_hubs(left_side):
+        if outgoing:
+            left, right = left_side.transpose(2, 0, 1), right_side.transpose(2, 1, 0)
+        else:
+            left, right = left_side.transpose(2, 1, 0), right_side.transpose(2, 0, 1)
+        return hub_sums(left, right, outgoing).transpose(1, 2, 0).astype(jnp.float32)
     if outgoing:
         return panels_outgoing(left_side, right_side)
     return panels_incoming(left_side, right_side)

time: 1150 us -> 821 us (0.71)
  waiting for transfers between devices: 793 us -> 0 us
  Pallas kernels: 0 us -> 477 us
  matrix products: 118 us -> 54.8 us
  other arithmetic: 60.4 us -> 94.4 us
  local copies, waits for them, and re-layouts: 160 us -> 184 us
  between operations: 13.6 us -> 0.7 us
    pallas_call x0 -> x2, Pallas kernels: none -> 477 us  [hub_sums(): pl.pallas_call(functools.partial(triangle_kernel, outgoing, half, step),...]
    all_gather x2 -> x0, waiting for transfers between devices: 398 us -> none  [the longest x1 289 us: panels_outgoing(): right_panel = lax.all_gather(right_side, 'row', axis=0, tiled=True)]
    unnamed x6 -> x0, waiting for transfers between devices: 396 us -> none
    dot_general x2 -> x0, matrix products: 51 us -> none  [the longest x1 35.2 us: partial_sum(): jnp.einsum('kih,kjh->ijh', left_panel, right_side, preferred_element_type...]
    slice x0 -> x2, local copies, waits for them, and re-layouts: none -> 49.4 us  [the longest x1 24.7 us: run_pass(): projected[:, :, :hidden]]
    unnamed x33 -> x35, local copies, waits for them, and re-layouts: 118 us -> 82.8 us
    transpose x0 -> x2, other arithmetic: none -> 33.2 us  [the longest x1 16.6 us: triangle_sums(): left, right = (left_side.transpose(2, 1, 0), right_side.transpose(2, 0, 1))]
    all_gather x1 -> x0, local copies, waits for them, and re-layouts: 21.6 us -> none  [panels_outgoing(): right_panel = lax.all_gather(right_side, 'row', axis=0, tiled=True)]
  transfers between devices with their start and end apart: 4 -> 0, of which waited for: 4 -> 0; matrix products, arithmetic and copies ran while one was open for 1% -> 0% of each run, Pallas kernels for 0% -> 0%
where the time goes in v1:
time: 821 us; the launch traced here: 811 us
  Pallas kernels  477 us (58%)
  local copies, waits for them, and re-layouts  184 us (22%)
  other arithmetic  94.4 us (11%)
  matrix products  54.8 us (7%)
    pallas_call x2, Pallas kernels, hub_sums(): pl.pallas_call(functools.partial(triangle_kernel, outgoing, half, step),...  477 us
    unnamed x35, local copies, waits for them, and re-layouts  82.8 us
    dot_general x2, matrix products, run_pass(): jnp.dot(normed, proj_weight[which_pass], preferred_element_type=jnp.float32)  30.9 us
    slice x1, local copies, waits for them, and re-layouts, run_pass(): projected[:, :, :hidden]  24.7 us
    slice x1, local copies, waits for them, and re-layouts, run_pass(): projected[:, :, 2 * hidden:3 * hidden]  24.7 us
    reduce_sum x4, other arithmetic, layer_norm(): center = values - jnp.mean(values, axis=-1, keepdims=True)  18.3 us
    transpose x1, other arithmetic, triangle_sums(): left, right = (left_side.transpose(2, 1, 0), right_side.transpose(2, 0, 1))  16.6 us
    transpose x1, other arithmetic, triangle_sums(): left, right = (left_side.transpose(2, 0, 1), right_side.transpose(2, 1, 0))  16.6 us

profile of v1, /device:TPU:1, one launch (start us, length us, event | category | flops | bytes accessed | tf_op | source)
XLA Modules:
  0.0 810.8 jit_solution(16234090102864197110)
XLA Ops:
  18.5 6.9 copy.13
  25.4 15.4 %fusion.39 = f32[128,128,512]{2,1,0:T(8,128)} fusion(bf16[128,128,128]{2,1,0:T(8,128)(2,1)} %copy.13, bf16[2,128,512]{2,1,0:T(8,128)(2,1)S(1)} %copy-done.6), kind=kOutput, calls=%fused_computation.56 | convolution fusion | flops 2147483648 | bytes 37879808 | tf_op jit(solution)/shard_map/dot_general | solution.py:391
  40.8 24.7 %fusion.59 = (f32[128,128,128]{2,1,0:T(8,128)}, f32[128,128,128]{2,1,0:T(8,128)}, f32[128,128,128]{2,1,0:T(8,128)}, f32[128,128,128]{2,1,0:T(8,128)}) fusion(f32[128,128,512]{2,1,0:T(8,128)} %fusion.39), kind=kLoop, calls=%fused_computation.101 | loop fusion | bytes 67108864 | tf_op jit(solution)/shard_map/slice | solution.py:394
  65.5 9.3 %copy.36 = f32[128,128,128]{1,0,2:T(8,128)} copy(f32[128,128,128]{2,1,0:T(8,128)} %get-tuple-element.13) | data formatting | bytes 16777216
  74.8 9.3 %copy.37 = f32[128,128,128]{1,0,2:T(8,128)} copy(f32[128,128,128]{2,1,0:T(8,128)} %get-tuple-element.12) | data formatting | bytes 16777216
  84.1 9.3 %copy.38 = f32[128,128,128]{1,0,2:T(8,128)} copy(f32[128,128,128]{2,1,0:T(8,128)} %get-tuple-element.11) | data formatting | bytes 16777216
  93.3 9.3 %copy.39 = f32[128,128,128]{1,0,2:T(8,128)} copy(f32[128,128,128]{2,1,0:T(8,128)} %get-tuple-element.14) | data formatting | bytes 16777216
  102.7 16.6 %fusion.34 = (bf16[128,128,128]{2,1,0:T(8,128)(2,1)}, bf16[128,128,128]{1,2,0:T(8,128)(2,1)}) fusion(f32[128,128,128]{1,0,2:T(8,128)} %copy.39, f32[128,128,128]{1,0,2:T(8,128)} %copy.38, f32[128,128]{1,0:T(8,128)S(1)} %convolution_maximum_fusion, f32[128,128,128]{1,0,2:T(8,128)} %copy.37, f32[128,128,128]{1,0,2:T(8,128)} %copy.36), kind=kLoop, calls=%fused_computation.50 | loop fusion | flops 25165824 | bytes 42008576 | tf_op jit(solution)/shard_map/transpose | solution.py:366
  125.6 239.2 %shard_map.100 = bf16[128,128,128]{2,1,0:T(8,128)(2,1)} custom-call(bf16[128,128,128]{2,1,0:T(8,128)(2,1)} %copy.20.moved_ref, bf16[128,128,128]{2,1,0:T(8,128)(2,1)} %get-tuple-element.17.fixed_ref), custom_call_target="tpu_custom_call" | custom-call | flops 8589934592 | bytes 12582912 | tf_op jit(solution)/shard_map/pallas_call | solution.py:321
  378.7 9.4 %convert_reduce_fusion = (f32[128,128]{1,0:T(8,128)S(1)}, bf16[128,128,128]{1,0,2:T(8,128)(2,1)S(1)}) fusion(f32[128,128,128]{1,2,0:T(8,128)S(1)} %fusion.31, f32[128,128,128]{1,2,0:T(8,128)S(1)} %fusion.45, bf16[128,128,128]{1,0,2:T(8,128)(2,1)S(1)} %copy-done.1), kind=kLoop, calls=%fused_computation.2 | loop fusion | flops 18857984 | bytes 25231360 | tf_op jit(solution)/shard_map/reduce_sum | solution.py:17
  390.1 13.1 %fusion.7 = bf16[128,128,128]{1,0,2:T(8,128)(2,1)} fusion(bf16[128,128,128]{1,0,2:T(8,128)(2,1)S(1)} %get-tuple-element.6, f32[128]{0:T(128)S(1)} %get-tuple-element.27, f32[128]{0:T(128)S(1)} %get-tuple-element.30, f32[128,128]{1,0:T(8,128)S(1)} %add_rsqrt_fusion.1, f32[128,128]{1,0:T(8,128)S(1)} %broadcast_multiply_fusion.1), kind=kLoop, calls=%fused_computation.13 | loop fusion | flops 12582912 | bytes 8520704 | tf_op jit(solution)/shard_map/convert_element_type | solution.py:390
  403.2 6.9 copy.24
  410.1 15.4 %fusion.37 = f32[128,128,512]{2,1,0:T(8,128)} fusion(bf16[128,128,128]{2,1,0:T(8,128)(2,1)} %copy.24, bf16[2,128,512]{2,1,0:T(8,128)(2,1)S(1)} %copy-done.6), kind=kOutput, calls=%fused_computation.54 | convolution fusion | flops 2147483648 | bytes 37879808 | tf_op jit(solution)/shard_map/dot_general | solution.py:391
  425.5 24.7 %fusion.58 = (f32[128,128,128]{2,1,0:T(8,128)}, f32[128,128,128]{2,1,0:T(8,128)}, f32[128,128,128]{2,1,0:T(8,128)}, f32[128,128,128]{2,1,0:T(8,128)}) fusion(f32[128,128,512]{2,1,0:T(8,128)} %fusion.37), kind=kLoop, calls=%fused_computation.100 | loop fusion | bytes 67108864 | tf_op jit(solution)/shard_map/slice | solution.py:398
  450.2 9.3 %copy.41 = f32[128,128,128]{1,0,2:T(8,128)} copy(f32[128,128,128]{2,1,0:T(8,128)} %get-tuple-element.9) | data formatting | bytes 16777216
  459.5 9.3 %copy.42 = f32[128,128,128]{1,0,2:T(8,128)} copy(f32[128,128,128]{2,1,0:T(8,128)} %get-tuple-element.8) | data formatting | bytes 16777216
  468.8 9.3 %copy.43 = f32[128,128,128]{1,0,2:T(8,128)} copy(f32[128,128,128]{2,1,0:T(8,128)} %get-tuple-element.7) | data formatting | bytes 16777216
  478.1 9.3 %copy.44 = f32[128,128,128]{1,0,2:T(8,128)} copy(f32[128,128,128]{2,1,0:T(8,128)} %get-tuple-element.10) | data formatting | bytes 16777216
  487.4 16.6 %fusion.36 = (bf16[128,128,128]{2,1,0:T(8,128)(2,1)}, bf16[128,128,128]{1,2,0:T(8,128)(2,1)}) fusion(f32[128,128,128]{1,0,2:T(8,128)} %copy.44, f32[128,128,128]{1,0,2:T(8,128)} %copy.43, f32[128,128]{1,0:T(8,128)S(1)} %convolution_maximum_fusion, f32[128,128,128]{1,0,2:T(8,128)} %copy.42, f32[128,128,128]{1,0,2:T(8,128)} %copy.41), kind=kLoop, calls=%fused_computation.52 | loop fusion | flops 25165824 | bytes 42008576 | tf_op jit(solution)/shard_map/transpose | solution.py:368
  510.3 237.5 %shard_map.101 = bf16[128,128,128]{2,1,0:T(8,128)(2,1)} custom-call(bf16[128,128,128]{2,1,0:T(8,128)(2,1)} %copy.31.moved_ref, bf16[128,128,128]{2,1,0:T(8,128)(2,1)} %get-tuple-element.15.fixed_ref), custom_call_target="tpu_custom_call" | custom-call | flops 8589934592 | bytes 12582912 | tf_op jit(solution)/shard_map/pallas_call | solution.py:321
  756.4 11.6 %fusion.29 = f32[128,128,128]{2,1,0:T(8,128)} fusion(bf16[128,128,128]{1,0,2:T(8,128)(2,1)S(1)} %fusion.19, bf16[2,128,128]{2,1,0:T(8,128)(2,1)S(1)} %copy-done.7), kind=kOutput, calls=%fused_computation.45 | convolution fusion | flops 536870912 | bytes 12615680 | tf_op jit(solution)/shard_map/dot_general | solution.py:408
  768.0 9.3 %copy.33 = f32[128,128,128]{1,0,2:T(8,128)} copy(f32[128,128,128]{2,1,0:T(8,128)} %fusion.29) | data formatting | bytes 16777216 | tf_op jit(solution)/shard_map/dot_general | solution.py:408
  783.9 9.3 %copy.25 = f32[128,128,128]{1,0,2:T(8,128)} copy(f32[128,128,128]{2,1,0:T(8,128)} %fusion.48) | data formatting | bytes 16777216 | tf_op jit(solution)/shard_map/dot_general | solution.py:406
  793.2 10.4 %fusion.13 = bf16[128,128,128]{1,0,2:T(8,128)(2,1)} fusion(bf16[128,128,128]{1,0,2:T(8,128)(2,1)} %copy-done.2, f32[128,128,128]{1,0,2:T(8,128)} %copy.33, f32[128,128,128]{1,0,2:T(8,128)} %copy.25), kind=kLoop, calls=%fused_computation.19 | loop fusion | flops 14680064 | bytes 25165824 | tf_op jit(solution)/shard_map/convert_element_type | solution.py:411
  (57 shorter events, 68.9 us)
Async XLA Ops:
  2.1 13.1 %copy-start.9 = (f32[2,128]{1,0:T(2,128)S(1)}, f32[2,128]{1,0:T(2,128)}, u32[]{:S(2)}) copy-start(f32[2,128]{1,0:T(2,128)} %param.14) | copy-start | bytes 3076
  2.1 13.1 %copy-start.10 = (f32[2,128]{1,0:T(2,128)S(1)}, f32[2,128]{1,0:T(2,128)}, u32[]{:S(2)}) copy-start(f32[2,128]{1,0:T(2,128)} %param.13) | copy-start | bytes 3076
  8.8 6.4 copy-start
  15.2 10.2 %copy-start.6 = (bf16[2,128,512]{2,1,0:T(8,128)(2,1)S(1)}, bf16[2,128,512]{2,1,0:T(8,128)(2,1)}, u32[]{:S(2)}) copy-start(bf16[2,128,512]{2,1,0:T(8,128)(2,1)} %param.15) | copy-start | bytes 786436
  364.9 6.4 copy-start.11
  364.9 6.4 copy-start.12
  364.9 6.4 copy-start.4
  364.9 8.4 %copy-start.7 = (bf16[2,128,128]{2,1,0:T(8,128)(2,1)S(1)}, bf16[2,128,128]{2,1,0:T(8,128)(2,1)}, u32[]{:S(2)}) copy-start(bf16[2,128,128]{2,1,0:T(8,128)(2,1)} %param.19) | copy-start | bytes 196612
  373.3 3.2 copy-start.3
  373.3 3.2 copy-start.8
  376.5 2.2 copy-start.1
  388.1 2.0 copy-start.2
  747.8 6.4 copy-start.5

commit v2 on v1

--- a/solution.py
+++ b/solution.py
@@ -187,16 +187,23 @@
             pl.semaphore_signal(barrier, inc=1, device_id=device, device_id_type=MESH)
         pl.semaphore_wait(barrier, 2)
 
-    def tile(group, e, b, h):
-        total = None
-        for v in range(2):
+    def product(lhs, rhs, dims):
+        return lax.dot_general(lhs, rhs, (dims, ((), ())), preferred_element_type=jnp.float32)
+
+    def tiles(group, h):
+        for e in range(2):
             if outgoing:
-                lhs, rhs = fixed[e, v, h], moved[2 * group + b, v, h]
+                lhs = [fixed[e, v, h] for v in range(2)]
             else:
-                lhs, rhs = moved[2 * group + e, v, h], fixed[b, v, h]
-            term = jnp.dot(lhs, rhs, preferred_element_type=jnp.float32)
-            total = term if total is None else total + term
-        return total
+                lhs = [moved[2 * group + e, v, h].T for v in range(2)]
+            for b in range(2):
+                if outgoing:
+                    terms = [
+                        product(lhs[v], moved[2 * group + b, v, h], ((1,), (1,))) for v in range(2)
+                    ]
+                else:
+                    terms = [product(lhs[v], fixed[b, v, h], ((1,), (0,))) for v in range(2)]
+                yield e, b, terms[0] + terms[1]
 
     @pl.when(edge)
     def _():
@@ -261,19 +268,15 @@
 
                 @pl.loop(0, step)
                 def _(h):
-                    for e in range(2):
-                        for b in range(2):
-                            sent[n % 2, h, e, b] = tile(1 - mine, e, b, n * step + h).astype(
-                                jnp.bfloat16
-                            )
+                    for e, b, total in tiles(1 - mine, n * step + h):
+                        sent[n % 2, h, e, b] = total.astype(jnp.bfloat16)
 
                 sums_to(n).start()
 
                 @pl.loop(0, step)
                 def _(h):
-                    for e in range(2):
-                        for b in range(2):
-                            summed[n % 2, h, e, b] = tile(mine, e, b, n * step + h)
+                    for e, b, total in tiles(mine, n * step + h):
+                        summed[n % 2, h, e, b] = total
 
             n = g - 2
             if 0 <= n < CHUNKS:
@@ -349,24 +352,120 @@
     )(moved, fixed)
 
 
-def takes_hubs(left_side):
-    rows, cols, hidden = left_side.shape
+ROWS = 16
+
+
+def sigmoid(values):
+    return 0.5 * jnp.tanh(0.5 * values) + 0.5
+
+
+def norm_rows(values, gain, shift):
+    center = values - jnp.mean(values, axis=-1, keepdims=True)
+    spread = jnp.mean(center * center, axis=-1, keepdims=True)
+    return center * lax.rsqrt(spread + EPSILON) * gain + shift
+
+
+def sides_kernel(x_ref, mask_ref, gain_ref, shift_ref, weight_ref, left_ref, right_ref, a_ref, b_ref):
+    hidden = left_ref.shape[0]
+    for row in range(ROWS):
+        normed = norm_rows(x_ref[row].astype(jnp.float32), gain_ref[...], shift_ref[...])
+        projected = lax.dot_general(
+            weight_ref[...], normed.astype(jnp.bfloat16), (((1,), (1,)), ((), ())),
+            preferred_element_type=jnp.float32,
+        )
+        masked = mask_ref[row : row + 1, :]
+        place = pl.ds(row, hidden, stride=ROWS)
+        a_ref[place, :] = masked * sigmoid(projected[:hidden]) * projected[hidden : 2 * hidden]
+        b_ref[place, :] = masked * sigmoid(projected[2 * hidden : 3 * hidden]) * projected[3 * hidden :]
+    shape = left_ref.shape
+    left_ref[...] = a_ref[...].astype(jnp.bfloat16).reshape(shape)
+    right_ref[...] = b_ref[...].astype(jnp.bfloat16).reshape(shape)
+
+
+def make_sides(state, pair_mask, gain, shift, weight):
+    rows, cols, channels = state.shape
+    hidden = weight.shape[1] // 4
+    side = jax.ShapeDtypeStruct((hidden, rows, cols), jnp.bfloat16)
+    return pl.pallas_call(
+        sides_kernel,
+        grid=(rows // ROWS,),
+        in_specs=[
+            pl.BlockSpec((ROWS, cols, channels), lambda r: (r, 0, 0)),
+            pl.BlockSpec((ROWS, cols), lambda r: (r, 0)),
+            pl.BlockSpec((1, channels), lambda r: (0, 0)),
+            pl.BlockSpec((1, channels), lambda r: (0, 0)),
+            pl.BlockSpec((4 * hidden, channels), lambda r: (0, 0)),
+        ],
+        out_specs=[pl.BlockSpec((hidden, ROWS, cols), lambda r: (0, r, 0))] * 2,
+        out_shape=[side, side],
+        scratch_shapes=[pltpu.VMEM((hidden * ROWS, cols), jnp.float32)] * 2,
+        compiler_params=pltpu.CompilerParams(vmem_limit_bytes=32 * 1024 * 1024),
+    )(state, pair_mask, gain[None], shift[None], weight.T)
+
+
+def update_kernel(
+    x_ref, sums_ref, gain_ref, shift_ref, gate_ref, out_gain_ref, out_shift_ref, weight_ref,
+    out_ref, t_ref,
+):
+    hidden = sums_ref.shape[0]
+    t_ref[...] = sums_ref[...].reshape(t_ref.shape).astype(jnp.float32)
+    for row in range(ROWS):
+        widened = x_ref[row].astype(jnp.float32)
+        normed = norm_rows(widened, gain_ref[...], shift_ref[...]).astype(jnp.bfloat16)
+        gating = sigmoid(
+            jnp.dot(normed, gate_ref[...], preferred_element_type=jnp.float32)
+        )
+        sums = t_ref[pl.ds(row, hidden, stride=ROWS), :]
+        center = sums - jnp.mean(sums, axis=0, keepdims=True)
+        spread = jnp.mean(center * center, axis=0, keepdims=True)
+        scaled = center * lax.rsqrt(spread + EPSILON)
+        tri_normed = (scaled * out_gain_ref[...] + out_shift_ref[...]).astype(jnp.bfloat16)
+        update = gating * jnp.dot(
+            tri_normed.T, weight_ref[...], preferred_element_type=jnp.float32
+        )
+        out_ref[row] = (widened + update).astype(jnp.bfloat16)
+
+
+def make_update(state, sums, gain, shift, gate, out_gain, out_shift, weight):
+    rows, cols, channels = state.shape
+    hidden = sums.shape[0]
+
+    def whole(*dims):
+        return pl.BlockSpec(dims, lambda r: (0,) * len(dims))
+
+    return pl.pallas_call(
+        update_kernel,
+        grid=(rows // ROWS,),
+        in_specs=[
+            pl.BlockSpec((ROWS, cols, channels), lambda r: (r, 0, 0)),
+            pl.BlockSpec((hidden, ROWS, cols), lambda r: (0, r, 0)),
+            whole(1, channels),
+            whole(1, channels),
+            whole(channels, channels),
+            whole(hidden, 1),
+            whole(hidden, 1),
+            whole(hidden, channels),
+        ],
+        out_specs=pl.BlockSpec((ROWS, cols, channels), lambda r: (r, 0, 0)),
+        out_shape=jax.ShapeDtypeStruct(state.shape, jnp.bfloat16),
+        scratch_shapes=[pltpu.VMEM((hidden * ROWS, cols), jnp.float32)],
+        compiler_params=pltpu.CompilerParams(vmem_limit_bytes=32 * 1024 * 1024),
+    )(state, sums, gain[None], shift[None], gate, out_gain[:, None], out_shift[:, None], weight)
+
+
+def takes_hubs(state, hidden):
+    rows, cols, channels = state.shape
     return (
         lax.axis_size("row") == 4
         and lax.axis_size("col") == 4
         and rows == cols
         and rows % 128 == 0
-        and hidden % (2 * CHUNKS) == 0
+        and channels % 128 == 0
+        and hidden % 128 == 0
     )
 
 
 def triangle_sums(left_side, right_side, outgoing):
-    if takes_hubs(left_side):
-        if outgoing:
-            left, right = left_side.transpose(2, 0, 1), right_side.transpose(2, 1, 0)
-        else:
-            left, right = left_side.transpose(2, 1, 0), right_side.transpose(2, 0, 1)
-        return hub_sums(left, right, outgoing).transpose(1, 2, 0).astype(jnp.float32)
     if outgoing:
         return panels_outgoing(left_side, right_side)
     return panels_incoming(left_side, right_side)
@@ -386,6 +485,14 @@
     outgoing,
 ):
     hidden = out_gain.shape[1]
+    if takes_hubs(state, hidden):
+        gain, shift = norm_gain[which_pass], norm_bias[which_pass]
+        left, right = make_sides(state, pair_mask, gain, shift, proj_weight[which_pass])
+        sums = hub_sums(left, right, outgoing)
+        return make_update(
+            state, sums, gain, shift, gate_weight[which_pass],
+            out_gain[which_pass], out_bias[which_pass], out_weight[which_pass],
+        )
     widened = state.astype(jnp.float32)
     normed = layer_norm(widened, norm_gain[which_pass], norm_bias[which_pass]).astype(jnp.bfloat16)
     projected = jnp.dot(normed, proj_weight[which_pass], preferred_element_type=jnp.float32)

time: 821 us -> 595 us (0.72); the launches traced: 811 us -> 595 us
  local copies, waits for them, and re-layouts: 184 us -> 25.5 us
  other arithmetic: 94.4 us -> 0.84 us
  Pallas kernels: 477 us -> 567 us
  matrix products: 54.8 us -> 1.19 us
    pallas_call x0 -> x4, Pallas kernels: none -> 89.5 us  [the longest x2 55.2 us: make_update(): pl.pallas_call(update_kernel, grid=(rows // ROWS,), in_specs=[pl.BlockSpe...]
    unnamed x35 -> x32, local copies, waits for them, and re-layouts: 82.8 us -> 23.2 us
    dot_general x6 -> x0, matrix products: 53.6 us -> none  [the longest x2 30.9 us: run_pass(): jnp.dot(normed, proj_weight[which_pass], preferred_element_type=jnp.float32)]
    slice x2, local copies, waits for them, and re-layouts: 49.4 us -> 1.77 us  [the longest x1 0.98 us: run_pass(): proj_weight[which_pass]]
    transpose x2 -> x0, other arithmetic: 33.2 us -> none  [the longest x1 16.6 us: triangle_sums(): left, right = (left_side.transpose(2, 1, 0), right_side.transpose(2, 0, 1))]
    convert_element_type x5 -> x0, other arithmetic: 30.9 us -> none  [the longest x2 16.3 us: run_pass(): layer_norm(widened, norm_gain[which_pass], norm_bias[which_pass])]
    reduce_sum x8 -> x0, other arithmetic: 29.4 us -> none  [the longest x4 18.3 us: layer_norm(): center = values - jnp.mean(values, axis=-1, keepdims=True)]
    convert_element_type x3 -> x0, local copies, waits for them, and re-layouts: 20.7 us -> none  [the longest x2 13.8 us: run_pass(): layer_norm(widened, norm_gain[which_pass], norm_bias[which_pass])]
where the time goes in v2:
time: 595 us
  Pallas kernels  567 us (95%)
  local copies, waits for them, and re-layouts  25.5 us (4%)
    pallas_call x2, Pallas kernels, hub_sums(): pl.pallas_call(functools.partial(triangle_kernel, outgoing, half, step),...  478 us
    pallas_call x2, Pallas kernels, make_update(): pl.pallas_call(update_kernel, grid=(rows // ROWS,), in_specs=[pl.BlockSpe...  55.2 us
    pallas_call x2, Pallas kernels, make_sides(): pl.pallas_call(sides_kernel, grid=(rows // ROWS,), in_specs=[pl.BlockSpec...  34.3 us
    unnamed x32, local copies, waits for them, and re-layouts  23.2 us

profile of v2, /device:TPU:1, one launch (start us, length us, event | category | flops | bytes accessed | tf_op | source)
XLA Modules:
  0.0 594.8 jit_solution(11942401496711522642)
XLA Ops:
  0.0 0.8 fusion.5
  0.8 0.9 fusion
  1.8 0.3 convolution_maximum_fusion.mask_ref
  2.1 0.8 fusion.6
  2.8 1.0 fusion.4
  3.8 0.1 copy.17
  4.0 2.2 copy-done.3
  6.1 17.2 %shard_map.100 = (bf16[128,128,128]{2,1,0:T(8,128)(2,1)S(1)}, bf16[128,128,128]{2,1,0:T(8,128)(2,1)S(1)}) custom-call(bf16[128,128,128]{2,1,0:T(8,128)(2,1)S(1)} %copy-done.3, f32[128,128]{1,0:T(8,128)S(1)} %convolution_maximum_fusion.mask_ref, f32[1,128]{1,0:T(1,128)S(1)} %get-tuple-element.30.gain_ref, f32[1,128]{1,0:T(1,128)S(1)} %get-tuple-element.26.shift_ref, ...), custom_call_target="tpu_custom_call" | custom-call | tf_op jit(solution)/shard_map/pallas_call | solution.py:389
  23.3 1.9 copy-done.9
  25.3 2.0 copy-done.10
  27.3 239.8 %shard_map.101.sums_ref = bf16[128,128,128]{2,1,0:T(8,128)(2,1)} custom-call(bf16[128,128,128]{2,1,0:T(8,128)(2,1)} %copy-done.10, bf16[128,128,128]{2,1,0:T(8,128)(2,1)} %copy-done.9), custom_call_target="tpu_custom_call" | custom-call | flops 8589934592 | bytes 12582912 | tf_op jit(solution)/shard_map/pallas_call | solution.py:324
  267.4 2.2 copy-done.4
  269.5 2.2 copy-done.5
  271.7 27.2 %shard_map.102.x_ref = bf16[128,128,128]{2,1,0:T(8,128)(2,1)S(1)} custom-call(bf16[128,128,128]{2,1,0:T(8,128)(2,1)S(1)} %copy-done.4, bf16[128,128,128]{2,1,0:T(8,128)(2,1)S(1)} %copy-done.5, f32[1,128]{1,0:T(1,128)S(1)} %get-tuple-element.30.gain_ref, f32[1,128]{1,0:T(1,128)S(1)} %get-tuple-element.26.shift_ref, ...), custom_call_target="tpu_custom_call" | custom-call | tf_op jit(solution)/shard_map/pallas_call | solution.py:436
  299.0 2.0 copy-done
  301.0 0.1 copy.18
  301.1 2.2 copy-done.1
  303.3 17.2 %shard_map.103 = (bf16[128,128,128]{2,1,0:T(8,128)(2,1)S(1)}, bf16[128,128,128]{2,1,0:T(8,128)(2,1)S(1)}) custom-call(bf16[128,128,128]{2,1,0:T(8,128)(2,1)S(1)} %copy-done.1, f32[128,128]{1,0:T(8,128)S(1)} %convolution_maximum_fusion.mask_ref, f32[1,128]{1,0:T(1,128)S(1)} %get-tuple-element.31.gain_ref, f32[1,128]{1,0:T(1,128)S(1)} %get-tuple-element.25.shift_ref, ...), custom_call_target="tpu_custom_call" | custom-call | tf_op jit(solution)/shard_map/pallas_call | solution.py:389
  320.4 1.9 copy-done.7
  322.4 2.0 copy-done.8
  324.4 237.8 %shard_map.104.sums_ref = bf16[128,128,128]{2,1,0:T(8,128)(2,1)} custom-call(bf16[128,128,128]{2,1,0:T(8,128)(2,1)} %copy-done.7, bf16[128,128,128]{2,1,0:T(8,128)(2,1)} %copy-done.8), custom_call_target="tpu_custom_call" | custom-call | flops 8589934592 | bytes 12582912 | tf_op jit(solution)/shard_map/pallas_call | solution.py:324
  562.4 2.2 copy-done.2
  564.6 2.2 copy-done.6
  566.8 28.0 %shard_map.105 = bf16[128,128,128]{2,1,0:T(8,128)(2,1)} custom-call(bf16[128,128,128]{2,1,0:T(8,128)(2,1)S(1)} %copy-done.2, bf16[128,128,128]{2,1,0:T(8,128)(2,1)S(1)} %copy-done.6, f32[1,128]{1,0:T(1,128)S(1)} %get-tuple-element.31.gain_ref, f32[1,128]{1,0:T(1,128)S(1)} %get-tuple-element.25.shift_ref, bf16[128,128]{1,0:T(8,128)(2,1)S(1)} %get-tuple-element.33.gate_ref, ...), custom_call_target="tpu_custom_call" | custom-call | tf_op jit(solution)/shard_map/pallas_call | solution.py:436
  (27 shorter events, 0.5 us)
Async XLA Ops:
  3.9 2.2 copy-start.3
  23.3 1.9 copy-start.9
  25.3 2.0 copy-start.10
  27.3 239.8 %copy-start.11 = (bf16[2,128,128]{2,1,0:T(8,128)(2,1)S(1)}, bf16[2,128,128]{2,1,0:T(8,128)(2,1)}, u32[]{:S(2)}) copy-start(bf16[2,128,128]{2,1,0:T(8,128)(2,1)} %param.19) | copy-start | bytes 196612
  27.3 239.8 %copy-start.12 = (bf16[2,128,128]{2,1,0:T(8,128)(2,1)S(1)}, bf16[2,128,128]{2,1,0:T(8,128)(2,1)}, u32[]{:S(2)}) copy-start(bf16[2,128,128]{2,1,0:T(8,128)(2,1)} %param.16) | copy-start | bytes 196612
  27.3 239.8 %copy-start.13 = (f32[2,128]{1,0:T(2,128)S(1)}, f32[2,128]{1,0:T(2,128)}, u32[]{:S(2)}) copy-start(f32[2,128]{1,0:T(2,128)} %param.17) | copy-start | bytes 3076
  27.3 239.9 %copy-start.14 = (f32[2,128]{1,0:T(2,128)S(1)}, f32[2,128]{1,0:T(2,128)}, u32[]{:S(2)}) copy-start(f32[2,128]{1,0:T(2,128)} %param.18) | copy-start | bytes 3076
  267.4 2.2 copy-start.4
  269.5 2.2 copy-start.5
  298.9 2.0 copy-start
  301.1 2.2 copy-start.1
  320.4 1.9 copy-start.7
  322.4 2.0 copy-start.8
  562.4 2.2 copy-start.2
  564.6 2.2 copy-start.6

commit v3 on v2

--- a/solution.py
+++ b/solution.py
@@ -73,7 +73,7 @@
 
 
 MESH = pl.DeviceIdType.MESH
-CHUNKS = 8
+CHUNKS = 16
 
 
 def triangle_kernel(
@@ -399,7 +399,7 @@
         out_specs=[pl.BlockSpec((hidden, ROWS, cols), lambda r: (0, r, 0))] * 2,
         out_shape=[side, side],
         scratch_shapes=[pltpu.VMEM((hidden * ROWS, cols), jnp.float32)] * 2,
-        compiler_params=pltpu.CompilerParams(vmem_limit_bytes=32 * 1024 * 1024),
+        compiler_params=pltpu.CompilerParams(vmem_limit_bytes=56 * 1024 * 1024),
     )(state, pair_mask, gain[None], shift[None], weight.T)
 
 
@@ -449,7 +449,7 @@
         out_specs=pl.BlockSpec((ROWS, cols, channels), lambda r: (r, 0, 0)),
         out_shape=jax.ShapeDtypeStruct(state.shape, jnp.bfloat16),
         scratch_shapes=[pltpu.VMEM((hidden * ROWS, cols), jnp.float32)],
-        compiler_params=pltpu.CompilerParams(vmem_limit_bytes=32 * 1024 * 1024),
+        compiler_params=pltpu.CompilerParams(vmem_limit_bytes=56 * 1024 * 1024),
     )(state, sums, gain[None], shift[None], gate, out_gain[:, None], out_shift[:, None], weight)
 
 

time: 595 us -> 538 us (0.904)
  Pallas kernels: 567 us -> 528 us
  local copies, waits for them, and re-layouts: 25.5 us -> 7.47 us
    pallas_call x2, Pallas kernels: 478 us -> 434 us  [hub_sums(): pl.pallas_call(functools.partial(triangle_kernel, outgoing, half, step),...]
    unnamed x32 -> x10, local copies, waits for them, and re-layouts: 23.2 us -> 1.53 us
where the time goes in v3:
time: 538 us
  Pallas kernels  528 us (98%)
  local copies, waits for them, and re-layouts  7.47 us (1%)
    pallas_call x2, Pallas kernels, hub_sums(): pl.pallas_call(functools.partial(triangle_kernel, outgoing, half, step),...  434 us
    pallas_call x2, Pallas kernels, make_update(): pl.pallas_call(update_kernel, grid=(rows // ROWS,), in_specs=[pl.BlockSpe...  57.6 us
    pallas_call x2, Pallas kernels, make_sides(): pl.pallas_call(sides_kernel, grid=(rows // ROWS,), in_specs=[pl.BlockSpec...  36.5 us

profile of v3, /device:TPU:1, one launch (start us, length us, event | category | flops | bytes accessed | tf_op | source)
XLA Modules:
  0.0 538.1 jit_solution(9224840267745413588)
XLA Ops:
  0.0 0.8 fusion.5
  0.8 0.9 fusion
  1.8 0.9 convolution_maximum_fusion.mask_ref
  2.7 1.4 fusion.6
  4.0 1.0 fusion.4
  5.0 0.8 copy.17
  5.8 18.3 %shard_map.100 = (bf16[128,128,128]{2,1,0:T(8,128)(2,1)}, bf16[128,128,128]{2,1,0:T(8,128)(2,1)}) custom-call(bf16[128,128,128]{2,1,0:T(8,128)(2,1)} %x_ref.3, f32[128,128]{1,0:T(8,128)} %convolution_maximum_fusion.mask_ref, f32[1,128]{1,0:T(1,128)} %get-tuple-element.30.gain_ref, f32[1,128]{1,0:T(1,128)} %get-tuple-element.26.shift_ref, ...), custom_call_target="tpu_custom_call" | custom-call | tf_op jit(solution)/shard_map/pallas_call | solution.py:389
  24.1 0.0 copy-start.2
  24.1 0.0 copy-start.3
  24.1 217.6 %shard_map.101.sums_ref = bf16[128,128,128]{2,1,0:T(8,128)(2,1)} custom-call(bf16[128,128,128]{2,1,0:T(8,128)(2,1)} %get-tuple-element.9.moved_ref, bf16[128,128,128]{2,1,0:T(8,128)(2,1)} %get-tuple-element.10.fixed_ref), custom_call_target="tpu_custom_call" | custom-call | flops 8589934592 | bytes 12582912 | tf_op jit(solution)/shard_map/pallas_call | solution.py:324
  241.7 0.0 copy-done
  241.7 0.0 copy-done.1
  241.7 0.6 slice_bitcast_fusion
  242.3 0.0 copy-done.2
  242.3 0.7 copy.12.out_gain_ref
  243.1 0.0 copy-done.3
  243.1 0.7 copy.13.out_shift_ref
  243.8 28.8 %shard_map.102.x_ref = bf16[128,128,128]{2,1,0:T(8,128)(2,1)} custom-call(bf16[128,128,128]{2,1,0:T(8,128)(2,1)} %x_ref.3, bf16[128,128,128]{2,1,0:T(8,128)(2,1)} %shard_map.101.sums_ref, f32[1,128]{1,0:T(1,128)} %get-tuple-element.30.gain_ref, f32[1,128]{1,0:T(1,128)} %get-tuple-element.26.shift_ref, bf16[128,128]{1,0:T(8,128)(2,1)} %get-tuple-element.32.gate_ref, ...), custom_call_target="tpu_custom_call" | custom-call | tf_op jit(solution)/shard_map/pallas_call | solution.py:436
  272.6 0.8 copy.18
  273.4 18.3 %shard_map.103 = (bf16[128,128,128]{2,1,0:T(8,128)(2,1)}, bf16[128,128,128]{2,1,0:T(8,128)(2,1)}) custom-call(bf16[128,128,128]{2,1,0:T(8,128)(2,1)} %shard_map.102.x_ref, f32[128,128]{1,0:T(8,128)} %convolution_maximum_fusion.mask_ref, f32[1,128]{1,0:T(1,128)} %get-tuple-element.31.gain_ref, f32[1,128]{1,0:T(1,128)} %get-tuple-element.25.shift_ref, ...), custom_call_target="tpu_custom_call" | custom-call | tf_op jit(solution)/shard_map/pallas_call | solution.py:389
  291.6 216.2 %shard_map.104.sums_ref = bf16[128,128,128]{2,1,0:T(8,128)(2,1)} custom-call(bf16[128,128,128]{2,1,0:T(8,128)(2,1)} %get-tuple-element.11.moved_ref, bf16[128,128,128]{2,1,0:T(8,128)(2,1)} %get-tuple-element.12.fixed_ref), custom_call_target="tpu_custom_call" | custom-call | flops 8589934592 | bytes 12582912 | tf_op jit(solution)/shard_map/pallas_call | solution.py:324
  507.8 0.7 copy.15.out_gain_ref
  508.5 0.7 copy.16.out_shift_ref
  509.3 28.8 %shard_map.105 = bf16[128,128,128]{2,1,0:T(8,128)(2,1)} custom-call(bf16[128,128,128]{2,1,0:T(8,128)(2,1)} %shard_map.102.x_ref, bf16[128,128,128]{2,1,0:T(8,128)(2,1)} %shard_map.104.sums_ref, f32[1,128]{1,0:T(1,128)} %get-tuple-element.31.gain_ref, f32[1,128]{1,0:T(1,128)} %get-tuple-element.25.shift_ref, bf16[128,128]{1,0:T(8,128)(2,1)} %get-tuple-element.33.gate_ref, ...), custom_call_target="tpu_custom_call" | custom-call | tf_op jit(solution)/shard_map/pallas_call | solution.py:436
  (5 shorter events, 0.0 us)
Async XLA Ops:
  24.0 217.6 %copy-start = (bf16[2,128,128]{2,1,0:T(8,128)(2,1)S(1)}, bf16[2,128,128]{2,1,0:T(8,128)(2,1)}, u32[]{:S(2)}) copy-start(bf16[2,128,128]{2,1,0:T(8,128)(2,1)} %param.19) | copy-start | bytes 196612
  24.0 217.6 %copy-start.1 = (bf16[2,128,128]{2,1,0:T(8,128)(2,1)S(1)}, bf16[2,128,128]{2,1,0:T(8,128)(2,1)}, u32[]{:S(2)}) copy-start(bf16[2,128,128]{2,1,0:T(8,128)(2,1)} %param.16) | copy-start | bytes 196612
  24.1 218.3 %copy-start.2 = (f32[2,128]{1,0:T(2,128)S(1)}, f32[2,128]{1,0:T(2,128)}, u32[]{:S(2)}) copy-start(f32[2,128]{1,0:T(2,128)} %param.17) | copy-start | bytes 3076
  24.1 219.0 %copy-start.3 = (f32[2,128]{1,0:T(2,128)S(1)}, f32[2,128]{1,0:T(2,128)}, u32[]{:S(2)}) copy-start(f32[2,128]{1,0:T(2,128)} %param.18) | copy-start | bytes 3076

commit v4 on v3

--- a/solution.py
+++ b/solution.py
@@ -73,7 +73,7 @@
 
 
 MESH = pl.DeviceIdType.MESH
-CHUNKS = 16
+CHUNKS = 32
 
 
 def triangle_kernel(
@@ -208,15 +208,15 @@
     @pl.when(edge)
     def _():
         for g in range(CHUNKS):
-            if g >= 2:
+            if g >= 4:
                 for b in range(2):
-                    end_moved(g - 2, b).wait_send()
-                    end_fixed(g - 2, b).wait_send()
+                    end_moved(g - 4, b).wait_send()
+                    end_fixed(g - 4, b).wait_send()
             for b in range(2):
                 end_moved(g, b).start()
             for b in range(2):
                 end_fixed(g, b).start()
-        for g in range(CHUNKS - 2, CHUNKS):
+        for g in range(CHUNKS - 4, CHUNKS):
             for b in range(2):
                 end_moved(g, b).wait_send()
                 end_fixed(g, b).wait_send()

time: 538 us -> 521 us (0.968)
  Pallas kernels: 528 us -> 511 us
    pallas_call x2, Pallas kernels: 434 us -> 417 us  [hub_sums(): pl.pallas_call(functools.partial(triangle_kernel, outgoing, half, step),...]
where the time goes in v4:
time: 521 us
  Pallas kernels  511 us (98%)
  local copies, waits for them, and re-layouts  7.45 us (1%)
    pallas_call x2, Pallas kernels, hub_sums(): pl.pallas_call(functools.partial(triangle_kernel, outgoing, half, step),...  417 us
    pallas_call x2, Pallas kernels, make_update(): pl.pallas_call(update_kernel, grid=(rows // ROWS,), in_specs=[pl.BlockSpe...  57.6 us
    pallas_call x2, Pallas kernels, make_sides(): pl.pallas_call(sides_kernel, grid=(rows // ROWS,), in_specs=[pl.BlockSpec...  36.5 us

profile of v4, /device:TPU:1, one launch (start us, length us, event | category | flops | bytes accessed | tf_op | source)
XLA Modules:
  0.0 521.0 jit_solution(13904953753380524280)
XLA Ops:
  0.0 0.8 fusion.5
  0.8 0.9 fusion
  1.8 0.9 convolution_maximum_fusion.mask_ref
  2.7 1.4 fusion.6
  4.0 1.0 fusion.4
  5.0 0.8 copy.17
  5.8 18.3 %shard_map.100 = (bf16[128,128,128]{2,1,0:T(8,128)(2,1)}, bf16[128,128,128]{2,1,0:T(8,128)(2,1)}) custom-call(bf16[128,128,128]{2,1,0:T(8,128)(2,1)} %x_ref.3, f32[128,128]{1,0:T(8,128)} %convolution_maximum_fusion.mask_ref, f32[1,128]{1,0:T(1,128)} %get-tuple-element.30.gain_ref, f32[1,128]{1,0:T(1,128)} %get-tuple-element.26.shift_ref, ...), custom_call_target="tpu_custom_call" | custom-call | tf_op jit(solution)/shard_map/pallas_call | solution.py:389
  24.0 0.0 copy-start.2
  24.1 0.0 copy-start.3
  24.1 209.2 %shard_map.101.sums_ref = bf16[128,128,128]{2,1,0:T(8,128)(2,1)} custom-call(bf16[128,128,128]{2,1,0:T(8,128)(2,1)} %get-tuple-element.9.moved_ref, bf16[128,128,128]{2,1,0:T(8,128)(2,1)} %get-tuple-element.10.fixed_ref), custom_call_target="tpu_custom_call" | custom-call | flops 8589934592 | bytes 12582912 | tf_op jit(solution)/shard_map/pallas_call | solution.py:324
  233.2 0.0 copy-done
  233.3 0.0 copy-done.1
  233.3 0.6 slice_bitcast_fusion
  233.9 0.0 copy-done.2
  233.9 0.7 copy.12.out_gain_ref
  234.7 0.0 copy-done.3
  234.7 0.7 copy.13.out_shift_ref
  235.4 28.8 %shard_map.102.x_ref = bf16[128,128,128]{2,1,0:T(8,128)(2,1)} custom-call(bf16[128,128,128]{2,1,0:T(8,128)(2,1)} %x_ref.3, bf16[128,128,128]{2,1,0:T(8,128)(2,1)} %shard_map.101.sums_ref, f32[1,128]{1,0:T(1,128)} %get-tuple-element.30.gain_ref, f32[1,128]{1,0:T(1,128)} %get-tuple-element.26.shift_ref, bf16[128,128]{1,0:T(8,128)(2,1)} %get-tuple-element.32.gate_ref, ...), custom_call_target="tpu_custom_call" | custom-call | tf_op jit(solution)/shard_map/pallas_call | solution.py:436
  264.2 0.8 copy.18
  265.0 18.2 %shard_map.103 = (bf16[128,128,128]{2,1,0:T(8,128)(2,1)}, bf16[128,128,128]{2,1,0:T(8,128)(2,1)}) custom-call(bf16[128,128,128]{2,1,0:T(8,128)(2,1)} %shard_map.102.x_ref, f32[128,128]{1,0:T(8,128)} %convolution_maximum_fusion.mask_ref, f32[1,128]{1,0:T(1,128)} %get-tuple-element.31.gain_ref, f32[1,128]{1,0:T(1,128)} %get-tuple-element.25.shift_ref, ...), custom_call_target="tpu_custom_call" | custom-call | tf_op jit(solution)/shard_map/pallas_call | solution.py:389
  283.2 207.5 %shard_map.104.sums_ref = bf16[128,128,128]{2,1,0:T(8,128)(2,1)} custom-call(bf16[128,128,128]{2,1,0:T(8,128)(2,1)} %get-tuple-element.11.moved_ref, bf16[128,128,128]{2,1,0:T(8,128)(2,1)} %get-tuple-element.12.fixed_ref), custom_call_target="tpu_custom_call" | custom-call | flops 8589934592 | bytes 12582912 | tf_op jit(solution)/shard_map/pallas_call | solution.py:324
  490.7 0.7 copy.15.out_gain_ref
  491.4 0.7 copy.16.out_shift_ref
  492.1 28.8 %shard_map.105 = bf16[128,128,128]{2,1,0:T(8,128)(2,1)} custom-call(bf16[128,128,128]{2,1,0:T(8,128)(2,1)} %shard_map.102.x_ref, bf16[128,128,128]{2,1,0:T(8,128)(2,1)} %shard_map.104.sums_ref, f32[1,128]{1,0:T(1,128)} %get-tuple-element.31.gain_ref, f32[1,128]{1,0:T(1,128)} %get-tuple-element.25.shift_ref, bf16[128,128]{1,0:T(8,128)(2,1)} %get-tuple-element.33.gate_ref, ...), custom_call_target="tpu_custom_call" | custom-call | tf_op jit(solution)/shard_map/pallas_call | solution.py:436
  (5 shorter events, 0.0 us)
Async XLA Ops:
  24.0 209.2 %copy-start = (bf16[2,128,128]{2,1,0:T(8,128)(2,1)S(1)}, bf16[2,128,128]{2,1,0:T(8,128)(2,1)}, u32[]{:S(2)}) copy-start(bf16[2,128,128]{2,1,0:T(8,128)(2,1)} %param.19) | copy-start | bytes 196612
  24.0 209.2 %copy-start.1 = (bf16[2,128,128]{2,1,0:T(8,128)(2,1)S(1)}, bf16[2,128,128]{2,1,0:T(8,128)(2,1)}, u32[]{:S(2)}) copy-start(bf16[2,128,128]{2,1,0:T(8,128)(2,1)} %param.16) | copy-start | bytes 196612
  24.0 209.9 %copy-start.2 = (f32[2,128]{1,0:T(2,128)S(1)}, f32[2,128]{1,0:T(2,128)}, u32[]{:S(2)}) copy-start(f32[2,128]{1,0:T(2,128)} %param.17) | copy-start | bytes 3076
  24.1 210.6 %copy-start.3 = (f32[2,128]{1,0:T(2,128)S(1)}, f32[2,128]{1,0:T(2,128)}, u32[]{:S(2)}) copy-start(f32[2,128]{1,0:T(2,128)} %param.18) | copy-start | bytes 3076
